TPU v7x, 512 devices: a whole 4x4x16 slice. The times are simulated.
512 devices in a mesh: tri: 64 (over y, z), sub: 8 (over x, core).
Axes of the slice: x: 4, y: 4, z: 16, core: 2. Of those that a mesh axis runs over, the one named last changes fastest.
Arguments:
- stored_tiles: float32 [64, 10, 512, 512], P('tri', None, 'sub'), may hold values from -190 to 190, as said below
- cell_owner: int32 [64], replicated, may hold values from 0 to 63, as said below
Outputs:
- updated: float32 [64, 10, 512, 512], P('tri', None, 'sub')
Inputs may be any that keep to these rules, and one draw needn't show every extreme that they name: `cell_owner`: a permutation of the indices of tri. `stored_tiles`: every tile whose row and column blocks are equal is skew-symmetric, every pivot met is invertible, and slots that hold no tile are zero.
All inputs are finite; a program needn't handle non-finite values.
Results may differ from a plain program's by a relative error of at most 0.00035.
Values may be sent and summed in bfloat16 or wider, within the bound.
A program may use at most 64 MiB of HBM per device.

v0:
```python
import math
import jax
import jax.numpy as jnp
import numpy as np
from jax import lax
from jax.sharding import Mesh
from jax.sharding import PartitionSpec as P

NB = 32
TRI = ("tri_0", "tri_1")


def in_order(tiles, dim):
    tiles = jnp.moveaxis(tiles, 0, dim)
    dims = tiles.shape
    return tiles.reshape(*dims[:dim], dims[dim] * dims[dim + 1], *dims[dim + 2 :])


def gather_in_order(x, axes, turns):
    tiles = x[None]
    for k in turns:
        tiles = lax.all_gather(tiles, axes[k], axis=0, tiled=True)
    block = [lax.axis_size(axes[k]) for k in reversed(turns)]
    tiles = tiles.reshape(*block, *x.shape)
    turned = sorted(range(len(turns)), key=lambda place: turns[len(turns) - 1 - place])
    return tiles.transpose(*turned, *range(len(turns), tiles.ndim)).reshape(-1, *x.shape)


def gather_axes(x, axes, turns, dim):
    return in_order(gather_in_order(x, axes, turns), dim)


def layout(groups, per_group):
    half_group = per_group // 2
    slot_count = per_group * (per_group + 1) // 2
    row_table = np.full((groups * groups, slot_count), -1, np.int32)
    col_table = np.full((groups * groups, slot_count), -1, np.int32)
    for first_group in range(groups):
        for second_group in range(groups):
            cell_index = first_group * groups + second_group
            for inner_row in range(per_group):
                if first_group == second_group:
                    for inner_column in range(inner_row + 1):
                        slot_index = inner_row * (inner_row + 1) // 2 + inner_column
                        row_table[cell_index, slot_index] = first_group * per_group + inner_row
                        col_table[cell_index, slot_index] = first_group * per_group + inner_column
                else:
                    for inner_column in range(half_group):
                        slot_index = inner_row * half_group + inner_column
                        if first_group > second_group:
                            row_table[cell_index, slot_index] = first_group * per_group + inner_row
                            col_table[cell_index, slot_index] = (
                                second_group * per_group + inner_column
                            )
                        else:
                            row_table[cell_index, slot_index] = second_group * per_group + inner_row
                            col_table[cell_index, slot_index] = (
                                first_group * per_group + half_group + inner_column
                            )
    return (row_table, col_table)


def shards(stored_tiles, cell_owner):
    tri_count = lax.axis_size(TRI)
    groups = math.isqrt(tri_count)
    per_group = NB // groups
    half_group = per_group // 2
    strip_rows = stored_tiles.shape[2]
    block_order = stored_tiles.shape[3]
    row_table, col_table = layout(groups, per_group)
    position = lax.axis_index(TRI)
    my_cell = jnp.sum(jnp.where(cell_owner == position, jnp.arange(tri_count, dtype=jnp.int32), 0))
    cell_down = my_cell // groups
    cell_across = my_cell % groups
    row_group = jnp.maximum(cell_down, cell_across)
    col_group = jnp.minimum(cell_down, cell_across)
    my_rows = jnp.asarray(row_table)[my_cell]
    my_cols = jnp.asarray(col_table)[my_cell]
    row_local = jnp.clip(my_rows - row_group * per_group, 0, per_group - 1)
    col_local = jnp.clip(my_cols - col_group * per_group, 0, per_group - 1)
    holders = cell_owner[jnp.arange(groups) * groups]
    highest = lax.Precision.HIGHEST
    current = stored_tiles[0]
    lower_slots = np.array([member * half_group for member in range(per_group)], np.int32)
    first_slots = np.array(
        [member * (member + 1) // 2 if member > 0 else 0 for member in range(per_group)], np.int32
    )
    keep_first = np.array([1.0 if member > 0 else 0.0 for member in range(per_group)], np.float32)
    from_lower = current[lower_slots]
    from_first = current[first_slots] * keep_first[:, None, None]
    holder_part = jnp.where(cell_down > 0, from_lower, from_first)
    holder_part = jnp.where(cell_across == 0, holder_part, 0.0).astype(jnp.bfloat16)
    pivot_slot = 0 // 2
    pivot_part = jnp.where(my_cell == 0, current[pivot_slot], 0.0)
    piece_size = holder_part.size // tri_count
    spread_panel = lax.all_to_all(
        holder_part.reshape(tri_count, piece_size), TRI, split_axis=0, concat_axis=0, tiled=True
    )
    spread_pivot = lax.all_to_all(
        pivot_part.astype(jnp.bfloat16), TRI, split_axis=0, concat_axis=0, tiled=True
    ).astype(pivot_part.dtype)
    picked_panel = spread_panel[holders][:, None, :]
    picked_pivot = spread_pivot[holders[0]][None, :]
    whole_panel = gather_axes(picked_panel, TRI, (0, 1), 1)
    whole_pivot = gather_axes(picked_pivot.astype(jnp.bfloat16), TRI, (0, 1), 0).astype(
        picked_pivot.dtype
    )
    panels = whole_panel.reshape(groups, per_group, strip_rows, block_order)
    own_strips = panels[row_group]
    other_strips = panels[col_group]
    pivot_block = lax.all_gather(
        whole_pivot.astype(jnp.bfloat16), "sub", axis=0, tiled=True
    ).astype(whole_pivot.dtype)
    partner = lax.all_gather(other_strips, "sub", axis=1, tiled=True)
    gram_matrix = jnp.dot(pivot_block.T, pivot_block, precision=highest)
    factor = jnp.linalg.cholesky(gram_matrix)
    inverse = jax.scipy.linalg.cho_solve((factor, True), pivot_block.T)
    scaled = jnp.einsum(
        "irk,kc->irc", own_strips.astype(jnp.float32), inverse, precision=highest
    ).astype(jnp.bfloat16)
    left_slots = scaled[row_local]
    right_slots = partner[col_local]
    update = jnp.einsum("qrk,qck->qrc", left_slots, right_slots, preferred_element_type=jnp.float32)
    live_slots = (my_rows > 0) & (my_cols > 0)
    current = current + jnp.where(live_slots[:, None, None], update, 0.0)
    return current[None]


def solution(mesh):
    torus = Mesh(mesh.devices.reshape(4, 16, mesh.shape["sub"]), ("tri_0", "tri_1", "sub"))
    return jax.shard_map(
        shards,
        mesh=torus,
        in_specs=(P(TRI, None, "sub", None), P()),
        out_specs=P(TRI, None, "sub", None),
        check_vma=False,
    )
```

profile of v0, /device:TPU:1, one launch (start us, length us, event | category | flops | bytes accessed | tf_op | source)
XLA Modules:
  0.0 323.7 jit_solution(5538113034983923474)
XLA Ops:
  6.5 1.4 fusion.56
  8.6 0.9 fusion.39
  10.6 0.6 reshape.305
  11.3 19.3 %all-to-all-start.1 = ((bf16[64,2,256]{2,1,0:T(2,128)(2,1)}), bf16[64,2,256]{2,1,0:T(2,128)(2,1)S(1)}, u32[]{:S(2)}, u32[]{:S(2)}) async-start(bf16[64,2,256]{2,1,0:T(2,128)(2,1)} %reshape.305), calls=%async_computation.1 | async-start | bytes 131072 | tf_op jit(solution)/shard_map/all_to_all | solution.py:99
  33.4 1.3 gather_fusion.2
  34.7 0.7 pad_clamp_fusion.4
  35.4 1.9 gather_fusion.1
  37.3 1.9 gather_fusion
  40.6 0.7 fusion.59
  41.3 0.7 and_bitcast_fusion
  42.2 0.7 fusion.60
  43.2 2.1 reduce.26
  45.2 0.9 reshape.307
  46.2 14.6 %all-to-all-start = ((bf16[64,2,1024]{2,1,0:T(2,128)(2,1)}), bf16[64,2,1024]{2,1,0:T(2,128)(2,1)S(1)}, u32[]{:S(2)}, u32[]{:S(2)}) async-start(bf16[64,2,1024]{2,1,0:T(2,128)(2,1)} %reshape.307), calls=%async_computation | async-start | bytes 524288 | tf_op jit(solution)/shard_map/all_to_all | solution.py:96
  60.9 8.8 %all_gather.20 = bf16[4,1,512]{2,1,0:T(2,128)(2,1)S(1)} all-gather(bf16[1,1,512]{2,1,0:T(2,128)(2,1)S(1)} %fusion.54), channel_id=1, replica_groups=mesh['tri_0'=4,'tri_1'=16,'sub'=8] {'tri_0'}, dimensions={0}, use_global_device_ids=true | all-gather | bytes 5120 | tf_op jit(solution)/shard_map/all_gather | solution.py:22
  69.7 23.8 %all_gather.21 = bf16[64,1,512]{2,1,0:T(2,128)(2,1)S(1)} all-gather(bf16[4,1,512]{2,1,0:T(2,128)(2,1)S(1)} %all_gather.20), channel_id=1, replica_groups=mesh['tri_0'=4,'tri_1'=16,'sub'=8] {'tri_1'}, dimensions={0}, use_global_device_ids=true | all-gather | bytes 69632 | tf_op jit(solution)/shard_map/all_gather | solution.py:22
  93.9 23.9 %all_gather.22 = bf16[512,512]{1,0:T(8,128)(2,1)S(1)} all-gather(bf16[64,512]{1,0:T(8,128)(2,1)S(1)} %bitcast.120), channel_id=1, replica_groups=mesh['tri_0'=4,'tri_1'=16,'sub'=8] {'sub'}, dimensions={0}, use_global_device_ids=true | all-gather | bytes 589824 | tf_op jit(solution)/shard_map/all_gather | solution.py:111
  118.9 1.0 copy-done.1
  119.9 11.7 %cholesky.104 = f32[128,128]{1,0:T(8,128)S(1)} custom-call(f32[128,128]{1,0:T(8,128)S(1)} %cholesky.266), custom_call_target="Cholesky" | custom-call | tf_op jit(solution)/shard_map/jit(cholesky)/cholesky | solution.py:116
  131.6 9.8 %custom-call.34 = f32[1,128,128]{1,2,0:T(8,128)S(1)} custom-call(f32[1,128,128]{2,1,0:T(8,128)S(1)} %get-tuple-element.32), custom_call_target="InvertDiagBlocksLowerTriangular" | custom-call | tf_op jit(solution)/shard_map/jit(cholesky)/cholesky | solution.py:116
  142.6 9.8 %all-gather = bf16[32,2048]{1,0:T(8,128)(2,1)} all-gather(bf16[8,2048]{1,0:T(8,128)(2,1)S(1)} %gather_fusion.3), channel_id=2, replica_groups=mesh['tri_0'=4,'tri_1'=16,'sub'=8] {'tri_0'}, dimensions={0}, use_global_device_ids=true | all-gather | bytes 163840 | tf_op jit(solution)/shard_map/all_gather | solution.py:22
  153.0 1.0 copy.32
  154.3 11.7 %cholesky.217 = f32[128,128]{1,0:T(8,128)S(1)} custom-call(f32[128,128]{1,0:T(8,128)S(1)} %cholesky.270), custom_call_target="Cholesky" | custom-call | tf_op jit(solution)/shard_map/jit(cholesky)/cholesky | solution.py:116
  166.1 9.8 %custom-call.35 = f32[1,128,128]{1,2,0:T(8,128)S(1)} custom-call(f32[1,128,128]{2,1,0:T(8,128)S(1)} %get-tuple-element.29), custom_call_target="InvertDiagBlocksLowerTriangular" | custom-call | tf_op jit(solution)/shard_map/jit(cholesky)/cholesky | solution.py:116
  176.6 11.7 %cholesky.238 = f32[128,128]{1,0:T(8,128)S(1)} custom-call(f32[128,128]{1,0:T(8,128)S(1)} %cholesky.275), custom_call_target="Cholesky" | custom-call | tf_op jit(solution)/shard_map/jit(cholesky)/cholesky | solution.py:116
  188.3 10.0 %custom-call.36 = f32[1,128,128]{1,2,0:T(8,128)S(1)} custom-call(f32[1,128,128]{2,1,0:T(8,128)S(1)} %get-tuple-element.26), custom_call_target="InvertDiagBlocksLowerTriangular" | custom-call | tf_op jit(solution)/shard_map/jit(cholesky)/cholesky | solution.py:116
  198.9 11.7 %cholesky.255 = f32[128,128]{1,0:T(8,128)S(1)} custom-call(f32[128,128]{1,0:T(8,128)S(1)} %convolution_subtract_fusion.8), custom_call_target="Cholesky" | custom-call | tf_op jit(solution)/shard_map/jit(cholesky)/cholesky | solution.py:116
  210.6 0.7 compare_reduce_fusion.2
  212.7 0.7 compare_reduce_fusion.1
  214.1 0.7 compare_reduce_fusion
  215.7 10.8 %while.1 = (s32[]{:T(128)}, f32[512,512]{1,0:T(8,128)S(1)}, s32[4,2]{0,1:T(2,128)S(1)}, f32[4,128,128]{2,1,0:T(8,128)}, s32[]{:T(128)}) while((s32[]{:T(128)}, f32[512,512]{1,0:T(8,128)S(1)}, s32[4,2]{0,1:T(2,128)S(1)}, f32[4,128,128]{2,1,0:T(8,128)}, s32[]{:T(128)}) %tuple.27), condition=%wide.while_cond, body=%wide.while_body.sunk | while | flops 2 | bytes 132705 | solution.py:117
  216.4 2.0 bitcast_dynamic-update-slice_fusion.2
  219.1 2.0 bitcast_dynamic-update-slice_fusion.2
  221.8 2.0 bitcast_dynamic-update-slice_fusion.2
  224.5 2.0 bitcast_dynamic-update-slice_fusion.2
  226.5 40.1 %custom-call.37 = f32[4,128,128]{1,2,0:T(8,128)S(1)} custom-call(f32[4,128,128]{2,1,0:T(8,128)} %get-tuple-element.12), custom_call_target="InvertDiagBlocksLowerTriangular" | custom-call | tf_op jit(solution)/shard_map/jit(_cho_solve)/triangular_solve | solution.py:117
  266.7 1.7 copy.27
  268.4 1.2 copy.28
  269.6 2.6 reshape_reshape.6
  272.2 1.7 constant_dynamic-slice_fusion.1
  273.9 1.2 fusion.35
  275.1 1.2 bitcast_convert_fusion
  278.0 0.6 convolution_subtract_fusion.5
  281.0 0.7 convolution_subtract_fusion.4
  282.1 1.6 convolution_convert_fusion
  284.3 21.5 %all-gather.7.cloned.1.call-done = bf16[1,4,512,512]{3,2,1,0:T(8,128)(2,1)} async-done(((bf16[1,4,64,512]{3,2,1,0:T(8,128)(2,1)}), bf16[1,4,512,512]{3,2,1,0:T(8,128)(2,1)}) %all-gather.7.cloned.1.call-update) | async-done | bytes 2097168 | tf_op jit(solution)/shard_map/all_gather | solution.py:114
  305.8 5.5 %gather_fusion.5 = bf16[10,512,512]{2,1,0:T(8,128)(2,1)} fusion(bf16[4,512,512]{2,1,0:T(8,128)(2,1)} %bitcast.112, s32[1024]{0:T(1024)S(1)} %pad_clamp_fusion), kind=kCustom, calls=%fused_computation.5 | custom fusion | bytes 10485800 | tf_op jit(solution)/shard_map/gather | solution.py:122
  311.4 5.2 %fusion.1 = f32[1,10,64,512]{3,2,1,0:T(8,128)} fusion(bf16[10,64,512]{2,1,0:T(8,128)(2,1)S(1)} %gather_fusion.4, bf16[10,512,512]{2,1,0:T(8,128)(2,1)} %gather_fusion.5, pred[10]{0:T(512)(128)(4,1)S(1)} %and_bitcast_fusion, f32[1,10,64,512]{3,2,1,0:T(8,128)S(1)} %copy-done), kind=kOutput, calls=%fused_computation.10 | convolution fusion | flops 336199680 | bytes 8519690 | tf_op jit(solution)/shard_map/qrk,qck->qrc/dot_general | solution.py:123
  (75 shorter events, 14.2 us)
Async XLA Ops:
  6.5 35.5 %copy-start.3 = (f32[4]{0:T(128)S(1)}, f32[4]{0:T(128)}, u32[]{:S(2)}) copy-start(f32[4]{0:T(128)} %constant.245) | copy-start | bytes 52
  11.3 34.9 %all-to-all-start.1 = ((bf16[64,2,256]{2,1,0:T(2,128)(2,1)}), bf16[64,2,256]{2,1,0:T(2,128)(2,1)S(1)}, u32[]{:S(2)}, u32[]{:S(2)}) async-start(bf16[64,2,256]{2,1,0:T(2,128)(2,1)} %reshape.305), calls=%async_computation.1 | async-start | bytes 131072 | tf_op jit(solution)/shard_map/all_to_all | solution.py:99
  46.2 95.4 %all-to-all-start = ((bf16[64,2,1024]{2,1,0:T(2,128)(2,1)}), bf16[64,2,1024]{2,1,0:T(2,128)(2,1)S(1)}, u32[]{:S(2)}, u32[]{:S(2)}) async-start(bf16[64,2,1024]{2,1,0:T(2,128)(2,1)} %reshape.307), calls=%async_computation | async-start | bytes 524288 | tf_op jit(solution)/shard_map/all_to_all | solution.py:96
  60.8 205.9 %all-gather.5.cloned.1.call-start = ((), (), s32[]{:S(2)}) async-start(), calls=%async_computation.2 | async-start | bytes 2228224 | tf_op jit(solution)/shard_map/all_gather | solution.py:22
  118.9 1.0 copy-start.1
  119.9 32.8 %copy-start.2 = (f32[512,512]{1,0:T(8,128)S(1)}, f32[512,512]{1,0:T(8,128)}, u32[]{:S(2)}) copy-start(f32[512,512]{1,0:T(8,128)} %copy-done.1) | copy-start | bytes 3145732
  152.4 153.4 %all-gather.7.cloned.1.call-start = ((), (), s32[]{:S(2)}) async-start(), calls=%async_computation.3 | async-start | bytes 2359296 | tf_op jit(solution)/shard_map/all_gather | solution.py:114
  305.8 5.6 %copy-start = (f32[1,10,64,512]{3,2,1,0:T(8,128)S(1)}, f32[1,10,64,512]{3,2,1,0:T(8,128)}, u32[]{:S(2)}) copy-start(f32[1,10,64,512]{3,2,1,0:T(8,128)} %param.9) | copy-start | bytes 3932164
Sparse Core Ops, SparseCore 0:
  152.6 63.2 all-gather.4
  274.0 31.7 all-gather.6
where the time goes:
time: 329 us; the launch traced here: 324 us
  other arithmetic  129 us (39%)
  blocking collectives  66.3 us (20%)
  local copies, waits for them, and re-layouts  34.9 us (11%)
  starting transfers between devices  34.1 us (10%)
  between operations  21.9 us (7%)
  waiting for transfers between devices  21.6 us (7%)
  matrix products  16.1 us (5%)
    another operation x14, other arithmetic, shards(): factor = jnp.linalg.cholesky(gram_matrix)  78.8 us
    all_gather x3, blocking collectives, gather_in_order(): tiles = lax.all_gather(tiles, axes[k], axis=0, tiled=True)  42.5 us
    another operation x3, other arithmetic, shards(): inverse = jax.scipy.linalg.cho_solve((factor, True), pivot_block.T)  40.3 us
    all_gather x1, blocking collectives, shards(): lax.all_gather(whole_pivot.astype(jnp.bfloat16), 'sub', axis=0, tiled=True)  23.9 us
    all_gather x1, waiting for transfers between devices, shards(): partner = lax.all_gather(other_strips, 'sub', axis=1, tiled=True)  21.5 us
    all_to_all x1, starting transfers between devices, shards(): lax.all_to_all(pivot_part.astype(jnp.bfloat16), TRI, split_axis=0, concat...  19.3 us
    all_to_all x1, starting transfers between devices, shards(): lax.all_to_all(holder_part.reshape(tri_count, piece_size), TRI, split_axi...  14.6 us
    another operation x12, local copies, waits for them, and re-layouts  10.8 us
  transfers between devices with their start and end apart: 4, of which 1 were waited for; matrix products, arithmetic and copies ran while one was open for 48% of the time, Pallas kernels for 0%

commit v1 on v0

--- a/solution.py
+++ b/solution.py
@@ -8,6 +8,27 @@
 
 NB = 32
 TRI = ("tri_0", "tri_1")
+
+
+def laid_out(blocks, dim):
+    blocks = jnp.moveaxis(blocks, 0, dim)
+    dims = blocks.shape
+    return blocks.reshape(*dims[:dim], dims[dim] * dims[dim + 1], *dims[dim + 2 :])
+
+
+def doubled(x, axis):
+    peers, index = (lax.axis_size(axis), lax.axis_index(axis))
+    blocks, bit = (x[None], 1)
+    while bit < peers:
+        theirs = lax.ppermute(blocks, axis, [(i, i ^ bit) for i in range(peers)])
+        low = index & bit == 0
+        blocks = jnp.concatenate([jnp.where(low, blocks, theirs), jnp.where(low, theirs, blocks)])
+        bit *= 2
+    return blocks
+
+
+def collect(shard, axis, dim):
+    return laid_out(doubled(shard, axis), dim)
 
 
 def in_order(tiles, dim):
@@ -108,9 +129,7 @@
     panels = whole_panel.reshape(groups, per_group, strip_rows, block_order)
     own_strips = panels[row_group]
     other_strips = panels[col_group]
-    pivot_block = lax.all_gather(
-        whole_pivot.astype(jnp.bfloat16), "sub", axis=0, tiled=True
-    ).astype(whole_pivot.dtype)
+    pivot_block = collect(whole_pivot.astype(jnp.bfloat16), "sub", 0).astype(whole_pivot.dtype)
     partner = lax.all_gather(other_strips, "sub", axis=1, tiled=True)
     gram_matrix = jnp.dot(pivot_block.T, pivot_block, precision=highest)
     factor = jnp.linalg.cholesky(gram_matrix)

time: 329 us -> 334 us (1.015)
  blocking collectives: 66.3 us -> 42.8 us
  starting transfers between devices: 34.1 us -> 54.1 us
  waiting for transfers between devices: 21.6 us -> 31.3 us
    all_gather x1 -> x0, blocking collectives: 23.9 us -> none  [shards(): lax.all_gather(whole_pivot.astype(jnp.bfloat16), 'sub', axis=0, tiled=True)]
    ppermute x0 -> x3, starting transfers between devices: none -> 20.3 us  [doubled(): theirs = lax.ppermute(blocks, axis, [(i, i ^ bit) for i in range(peers)])]
    ppermute x0 -> x3, waiting for transfers between devices: none -> 7.1 us  [doubled(): theirs = lax.ppermute(blocks, axis, [(i, i ^ bit) for i in range(peers)])]
  transfers between devices with their start and end apart: 4 -> 7, of which waited for: 1 -> 5; matrix products, arithmetic and copies ran while one was open for 48% -> 47% of each run, Pallas kernels for 0% -> 0%
where the time goes in v1:
time: 334 us; the launch traced here: 328 us
  other arithmetic  129 us (39%)
  starting transfers between devices  54.1 us (16%)
  blocking collectives  42.8 us (13%)
  local copies, waits for them, and re-layouts  34.1 us (10%)
  waiting for transfers between devices  31.3 us (9%)
  between operations  21.2 us (6%)
  matrix products  16.1 us (5%)
    another operation x14, other arithmetic, shards(): factor = jnp.linalg.cholesky(gram_matrix)  78.6 us
    all_gather x3, blocking collectives, gather_in_order(): tiles = lax.all_gather(tiles, axes[k], axis=0, tiled=True)  42.8 us
    another operation x3, other arithmetic, shards(): inverse = jax.scipy.linalg.cho_solve((factor, True), pivot_block.T)  40.3 us
    all_gather x1, waiting for transfers between devices, shards(): partner = lax.all_gather(other_strips, 'sub', axis=1, tiled=True)  23.8 us
    ppermute x3, starting transfers between devices, doubled(): theirs = lax.ppermute(blocks, axis, [(i, i ^ bit) for i in range(peers)])  20.3 us
    all_to_all x1, starting transfers between devices, shards(): lax.all_to_all(pivot_part.astype(jnp.bfloat16), TRI, split_axis=0, concat...  19.3 us
    all_to_all x1, starting transfers between devices, shards(): lax.all_to_all(holder_part.reshape(tri_count, piece_size), TRI, split_axi...  14.2 us
    another operation x12, local copies, waits for them, and re-layouts  10.6 us
  transfers between devices with their start and end apart: 7, of which 5 were waited for; matrix products, arithmetic and copies ran while one was open for 47% of the time, Pallas kernels for 0%

profile of v1, /device:TPU:1, one launch (start us, length us, event | category | flops | bytes accessed | tf_op | source)
XLA Modules:
  0.0 328.5 jit_solution(12710778907257383376)
XLA Ops:
  6.5 1.4 fusion.56
  8.5 0.9 fusion.39
  10.0 0.7 reduce.25
  11.4 19.3 %all-to-all-start.1 = ((bf16[64,2,256]{2,1,0:T(2,128)(2,1)}), bf16[64,2,256]{2,1,0:T(2,128)(2,1)S(1)}, u32[]{:S(2)}, u32[]{:S(2)}) async-start(bf16[64,2,256]{2,1,0:T(2,128)(2,1)} %reshape.311), calls=%async_computation.1 | async-start | bytes 131072 | tf_op jit(solution)/shard_map/all_to_all | solution.py:120
  33.3 1.3 gather_fusion.2
  35.9 1.9 gather_fusion.1
  37.9 1.9 gather_fusion
  40.1 2.2 reduce.26
  42.3 0.9 reshape.313
  44.2 14.2 %all-to-all-start = ((bf16[64,2,1024]{2,1,0:T(2,128)(2,1)}), bf16[64,2,1024]{2,1,0:T(2,128)(2,1)S(1)}, u32[]{:S(2)}, u32[]{:S(2)}) async-start(bf16[64,2,1024]{2,1,0:T(2,128)(2,1)} %reshape.313), calls=%async_computation | async-start | bytes 524288 | tf_op jit(solution)/shard_map/all_to_all | solution.py:117
  58.6 8.8 %all_gather.17 = bf16[4,1,512]{2,1,0:T(2,128)(2,1)S(1)} all-gather(bf16[1,1,512]{2,1,0:T(2,128)(2,1)S(1)} %fusion.54), channel_id=1, replica_groups=mesh['tri_0'=4,'tri_1'=16,'sub'=8] {'tri_0'}, dimensions={0}, use_global_device_ids=true | all-gather | bytes 5120 | tf_op jit(solution)/shard_map/all_gather | solution.py:43
  67.4 23.8 %all_gather.18 = bf16[64,1,512]{2,1,0:T(2,128)(2,1)S(1)} all-gather(bf16[4,1,512]{2,1,0:T(2,128)(2,1)S(1)} %all_gather.17), channel_id=1, replica_groups=mesh['tri_0'=4,'tri_1'=16,'sub'=8] {'tri_1'}, dimensions={0}, use_global_device_ids=true | all-gather | bytes 69632 | tf_op jit(solution)/shard_map/all_gather | solution.py:43
  91.6 12.0 %collective-permute-start = (bf16[1,64,512]{2,1,0:T(8,128)(2,1)S(1)}, bf16[1,64,512]{2,1,0:T(8,128)(2,1)S(1)}, u32[]{:S(2)}, u32[]{:S(2)}) collective-permute-start(bf16[1,64,512]{2,1,0:T(8,128)(2,1)S(1)} %bitcast.125), channel_id=1, source_target_pairs={{0,1},{1,0},{2,3},{3,2},{4,5},{5,4},{6,7},{7,6},{8,9},{9,8},{10,11... | collective-permute-start | bytes 196616 | tf_op jit(solution)/shard_map/ppermute | solution.py:23
  103.7 0.9 collective-permute-done
  104.6 3.1 collective-permute-start.1
  107.7 0.7 fusion.59
  108.4 2.8 collective-permute-done.1
  111.3 5.1 %collective-permute-start.2 = (bf16[4,64,512]{2,1,0:T(8,128)(2,1)S(1)}, bf16[4,64,512]{2,1,0:T(8,128)(2,1)S(1)}, u32[]{:S(2)}, u32[]{:S(2)}) collective-permute-start(bf16[4,64,512]{2,1,0:T(8,128)(2,1)S(1)} %pad_maximum_fusion.1), channel_id=1, source_target_pairs={{0,4},{1,5},{2,6},{3,7},{4,0},{5,1},{6,2},{7,3},{8,12},{9,13},{10,... | collective-permute-start | bytes 786440 | tf_op jit(solution)/shard_map/ppermute | solution.py:23
  116.4 0.7 fusion.60
  117.1 0.7 and_bitcast_fusion
  117.8 3.5 %collective-permute-done.2 = bf16[4,64,512]{2,1,0:T(8,128)(2,1)S(1)} collective-permute-done((bf16[4,64,512]{2,1,0:T(8,128)(2,1)S(1)}, bf16[4,64,512]{2,1,0:T(8,128)(2,1)S(1)}, u32[]{:S(2)}, u32[]{:S(2)}) %collective-permute-start.2) | collective-permute-done | bytes 262176 | tf_op jit(solution)/shard_map/ppermute | solution.py:23
  122.7 11.7 %cholesky.104 = f32[128,128]{1,0:T(8,128)S(1)} custom-call(f32[128,128]{1,0:T(8,128)S(1)} %cholesky.266), custom_call_target="Cholesky" | custom-call | tf_op jit(solution)/shard_map/jit(cholesky)/cholesky | solution.py:135
  134.6 9.8 %custom-call.34 = f32[1,128,128]{1,2,0:T(8,128)S(1)} custom-call(f32[1,128,128]{2,1,0:T(8,128)S(1)} %get-tuple-element.38), custom_call_target="InvertDiagBlocksLowerTriangular" | custom-call | tf_op jit(solution)/shard_map/jit(cholesky)/cholesky | solution.py:135
  145.7 10.1 %all-gather = bf16[32,2048]{1,0:T(8,128)(2,1)} all-gather(bf16[8,2048]{1,0:T(8,128)(2,1)S(1)} %gather_fusion.3), channel_id=2, replica_groups=mesh['tri_0'=4,'tri_1'=16,'sub'=8] {'tri_0'}, dimensions={0}, use_global_device_ids=true | all-gather | bytes 163840 | tf_op jit(solution)/shard_map/all_gather | solution.py:43
  156.5 11.7 %cholesky.217 = f32[128,128]{1,0:T(8,128)S(1)} custom-call(f32[128,128]{1,0:T(8,128)S(1)} %cholesky.270), custom_call_target="Cholesky" | custom-call | tf_op jit(solution)/shard_map/jit(cholesky)/cholesky | solution.py:135
  168.2 9.8 %custom-call.35 = f32[1,128,128]{1,2,0:T(8,128)S(1)} custom-call(f32[1,128,128]{2,1,0:T(8,128)S(1)} %get-tuple-element.35), custom_call_target="InvertDiagBlocksLowerTriangular" | custom-call | tf_op jit(solution)/shard_map/jit(cholesky)/cholesky | solution.py:135
  178.7 11.7 %cholesky.238 = f32[128,128]{1,0:T(8,128)S(1)} custom-call(f32[128,128]{1,0:T(8,128)S(1)} %cholesky.275), custom_call_target="Cholesky" | custom-call | tf_op jit(solution)/shard_map/jit(cholesky)/cholesky | solution.py:135
  190.5 10.0 %custom-call.36 = f32[1,128,128]{1,2,0:T(8,128)S(1)} custom-call(f32[1,128,128]{2,1,0:T(8,128)S(1)} %get-tuple-element.32), custom_call_target="InvertDiagBlocksLowerTriangular" | custom-call | tf_op jit(solution)/shard_map/jit(cholesky)/cholesky | solution.py:135
  201.1 11.7 %cholesky.255 = f32[128,128]{1,0:T(8,128)S(1)} custom-call(f32[128,128]{1,0:T(8,128)S(1)} %convolution_subtract_fusion.8), custom_call_target="Cholesky" | custom-call | tf_op jit(solution)/shard_map/jit(cholesky)/cholesky | solution.py:135
  212.8 0.7 compare_reduce_fusion.2
  217.4 10.6 %while.1 = (s32[]{:T(128)}, f32[512,512]{1,0:T(8,128)S(1)}, s32[4,2]{0,1:T(2,128)S(1)}, f32[4,128,128]{2,1,0:T(8,128)}, s32[]{:T(128)}) while((s32[]{:T(128)}, f32[512,512]{1,0:T(8,128)S(1)}, s32[4,2]{0,1:T(2,128)S(1)}, f32[4,128,128]{2,1,0:T(8,128)}, s32[]{:T(128)}) %tuple.30), condition=%wide.while_cond, body=%wide.while_body.sunk | while | flops 2 | bytes 132705 | solution.py:136
  218.1 2.0 bitcast_dynamic-update-slice_fusion.2
  220.7 2.0 bitcast_dynamic-update-slice_fusion.2
  223.4 2.0 bitcast_dynamic-update-slice_fusion.2
  226.0 2.0 bitcast_dynamic-update-slice_fusion.2
  228.0 40.1 %custom-call.37 = f32[4,128,128]{1,2,0:T(8,128)S(1)} custom-call(f32[4,128,128]{2,1,0:T(8,128)} %get-tuple-element.12), custom_call_target="InvertDiagBlocksLowerTriangular" | custom-call | tf_op jit(solution)/shard_map/jit(_cho_solve)/triangular_solve | solution.py:136
  268.2 1.0 copy.34
  269.2 1.7 copy.29
  270.9 1.2 copy.30
  272.1 2.6 reshape_reshape.4
  274.7 1.7 constant_dynamic-slice_fusion.1
  276.4 1.2 fusion.35
  277.6 1.2 bitcast_convert_fusion
  283.6 0.7 convolution_subtract_fusion.4
  284.6 1.6 convolution_convert_fusion
  286.8 23.8 %all-gather.7.cloned.1.call-done = bf16[1,4,512,512]{3,2,1,0:T(8,128)(2,1)} async-done(((bf16[1,4,64,512]{3,2,1,0:T(8,128)(2,1)}), bf16[1,4,512,512]{3,2,1,0:T(8,128)(2,1)}) %all-gather.7.cloned.1.call-update) | async-done | bytes 2097168 | tf_op jit(solution)/shard_map/all_gather | solution.py:133
  310.6 5.5 %gather_fusion.5 = bf16[10,512,512]{2,1,0:T(8,128)(2,1)} fusion(bf16[4,512,512]{2,1,0:T(8,128)(2,1)} %bitcast.115, s32[1024]{0:T(1024)S(1)} %pad_clamp_fusion), kind=kCustom, calls=%fused_computation.5 | custom fusion | bytes 10485800 | tf_op jit(solution)/shard_map/gather | solution.py:141
  316.2 5.2 %fusion.1 = f32[1,10,64,512]{3,2,1,0:T(8,128)} fusion(bf16[10,64,512]{2,1,0:T(8,128)(2,1)S(1)} %gather_fusion.4, bf16[10,512,512]{2,1,0:T(8,128)(2,1)} %gather_fusion.5, pred[10]{0:T(512)(128)(4,1)S(1)} %and_bitcast_fusion, f32[1,10,64,512]{3,2,1,0:T(8,128)S(1)} %copy-done), kind=kOutput, calls=%fused_computation.10 | convolution fusion | flops 336199680 | bytes 8519690 | tf_op jit(solution)/shard_map/qrk,qck->qrc/dot_general | solution.py:142
  (90 shorter events, 17.7 us)
Async XLA Ops:
  6.5 33.2 %copy-start.5 = (f32[4]{0:T(128)S(1)}, f32[4]{0:T(128)}, u32[]{:S(2)}) copy-start(f32[4]{0:T(128)} %constant.250) | copy-start | bytes 52
  11.4 32.8 %all-to-all-start.1 = ((bf16[64,2,256]{2,1,0:T(2,128)(2,1)}), bf16[64,2,256]{2,1,0:T(2,128)(2,1)S(1)}, u32[]{:S(2)}, u32[]{:S(2)}) async-start(bf16[64,2,256]{2,1,0:T(2,128)(2,1)} %reshape.311), calls=%async_computation.1 | async-start | bytes 131072 | tf_op jit(solution)/shard_map/all_to_all | solution.py:120
  44.2 100.5 %all-to-all-start = ((bf16[64,2,1024]{2,1,0:T(2,128)(2,1)}), bf16[64,2,1024]{2,1,0:T(2,128)(2,1)S(1)}, u32[]{:S(2)}, u32[]{:S(2)}) async-start(bf16[64,2,1024]{2,1,0:T(2,128)(2,1)} %reshape.313), calls=%async_computation | async-start | bytes 524288 | tf_op jit(solution)/shard_map/all_to_all | solution.py:117
  58.5 210.7 %all-gather.5.cloned.1.call-start = ((), (), s32[]{:S(2)}) async-start(), calls=%async_computation.2 | async-start | bytes 2228224 | tf_op jit(solution)/shard_map/all_gather | solution.py:43
  91.6 12.9 %collective-permute-start = (bf16[1,64,512]{2,1,0:T(8,128)(2,1)S(1)}, bf16[1,64,512]{2,1,0:T(8,128)(2,1)S(1)}, u32[]{:S(2)}, u32[]{:S(2)}) collective-permute-start(bf16[1,64,512]{2,1,0:T(8,128)(2,1)S(1)} %bitcast.125), channel_id=1, source_target_pairs={{0,1},{1,0},{2,3},{3,2},{4,5},{5,4},{6,7},{7,6},{8,9},{9,8},{10,11... | collective-permute-start | bytes 196616 | tf_op jit(solution)/shard_map/ppermute | solution.py:23
  104.6 6.6 %collective-permute-start.1 = (bf16[2,64,512]{2,1,0:T(8,128)(2,1)S(1)}, bf16[2,64,512]{2,1,0:T(8,128)(2,1)S(1)}, u32[]{:S(2)}, u32[]{:S(2)}) collective-permute-start(bf16[2,64,512]{2,1,0:T(8,128)(2,1)S(1)} %pad_maximum_fusion.2), channel_id=1, source_target_pairs={{0,2},{1,3},{2,0},{3,1},{4,6},{5,7},{6,4},{7,5},{8,10},{9,11},{10,... | collective-permute-start | bytes 393224 | tf_op jit(solution)/shard_map/ppermute | solution.py:23
  111.3 10.0 %collective-permute-start.2 = (bf16[4,64,512]{2,1,0:T(8,128)(2,1)S(1)}, bf16[4,64,512]{2,1,0:T(8,128)(2,1)S(1)}, u32[]{:S(2)}, u32[]{:S(2)}) collective-permute-start(bf16[4,64,512]{2,1,0:T(8,128)(2,1)S(1)} %pad_maximum_fusion.1), channel_id=1, source_target_pairs={{0,4},{1,5},{2,6},{3,7},{4,0},{5,1},{6,2},{7,3},{8,12},{9,13},{10,... | collective-permute-start | bytes 786440 | tf_op jit(solution)/shard_map/ppermute | solution.py:23
  121.3 0.7 copy-start.1
  121.3 0.8 copy-start.3
  155.9 154.7 %all-gather.7.cloned.1.call-start = ((), (), s32[]{:S(2)}) async-start(), calls=%async_computation.3 | async-start | bytes 2359296 | tf_op jit(solution)/shard_map/all_gather | solution.py:133
  178.7 89.4 %copy-start.2 = (bf16[4,64,512]{2,1,0:T(8,128)(2,1)S(1)}, bf16[4,64,512]{2,1,0:T(8,128)(2,1)}, u32[]{:S(2)}) copy-start(bf16[4,64,512]{2,1,0:T(8,128)(2,1)} %copy-done.1) | copy-start | bytes 786436
  178.7 89.4 %copy-start.4 = (bf16[4,64,512]{2,1,0:T(8,128)(2,1)S(1)}, bf16[4,64,512]{2,1,0:T(8,128)(2,1)}, u32[]{:S(2)}) copy-start(bf16[4,64,512]{2,1,0:T(8,128)(2,1)} %copy-done.3) | copy-start | bytes 786436
  310.6 5.6 %copy-start = (f32[1,10,64,512]{3,2,1,0:T(8,128)S(1)}, f32[1,10,64,512]{3,2,1,0:T(8,128)}, u32[]{:S(2)}) copy-start(f32[1,10,64,512]{3,2,1,0:T(8,128)} %param.9) | copy-start | bytes 3932164
Sparse Core Ops, SparseCore 0:
  156.0 65.5 all-gather.4
  276.5 34.0 all-gather.6
